TPU v7x, 32 devices: a whole 2x2x4 slice. The times are simulated.
32 devices in a mesh: row: 2 (over core), col: 8 (over z, x), layer: 2 (over y).
Axes of the slice: x: 2, y: 2, z: 4, core: 2. Of those that a mesh axis runs over, the one named last changes fastest.
Arguments:
- tile_values: float32 [2, 16, 2, 6, 128, 128], P('row', ('col', 'layer')), may hold values from -1.8 to 1.8
- tile_rows: int32 [2, 16, 2, 6], P('row', ('col', 'layer')), may hold values from 0 to 127, as said below
- tile_cols: int32 [2, 16, 2, 6], P('row', ('col', 'layer')), may hold values from 0 to 127, as said below
- tile_counts: int32 [2, 16, 2], P('row', ('col', 'layer')), may hold values from 1 to 6, as said below
- out_rows: int32 [2, 8, 2, 12], P('row', 'col'), may hold values from 0 to 127, as said below
- out_cols: int32 [2, 8, 2, 12], P('row', 'col'), may hold values from 0 to 127, as said below
Outputs:
- squared: float32 [2, 16, 12, 128, 128], P('row', ('col', 'layer'))
Inputs may be any that keep to these rules, and one draw needn't show every extreme that they name: `tile_rows`: entry [r, s, h, q] lies in row band r (the 64 block rows from r * 64), in a run of 8 block rows whose index is congruent to h modulo 2; within one list [r, s, h] the 6 slots have distinct rows. `tile_cols`: entry [r, s, h, q] lies in sub-band s: block columns s * 8 to s * 8 + 7. Slots q < tile_counts[r, s, h] of list [r, s, h] hold tiles; values and coordinates in later slots mean nothing. Some list holds 6 tiles in every draw. out_rows[r, c, l, o] and out_cols[r, c, l, o] place the o-th kept tile of row band r and sub-band c * 2 + l; the row lies in row band r, the column in that sub-band, and the 12 positions of one [r, c, l] are distinct. `out_cols`: see out_rows.
All inputs are finite; a program needn't handle non-finite values.
Results may differ from a plain program's by a relative error of at most 0.0003.
Values sent between devices are 32-bit elements; how exact they have to be, the bound alone decides.
A program may use at most 128 MiB of HBM per device.

v0:
```python
import jax
import jax.numpy as jnp
from jax import lax
from jax.sharding import PartitionSpec as P


def live_slots(counts, capacity):
    slot_ids = jnp.arange(capacity, dtype=jnp.int32)
    return slot_ids < counts[..., None]


def flatten_list(listed):
    values, list_rows, list_cols, counts = listed
    tile_order = values.shape[-1]
    capacity = values.shape[-3]
    live_mask = live_slots(counts, capacity)
    return (
        values.reshape(-1, tile_order, tile_order),
        list_rows.reshape(-1),
        list_cols.reshape(-1),
        live_mask.reshape(-1),
    )


def tile_products(running, one_shard, column_panel, target_rows, target_cols):
    left_values, left_rows, left_cols, left_live = one_shard
    right_values, right_rows, right_cols, right_live = column_panel
    left_hits = (left_live[None, :] & (left_rows[None, :] == target_rows[:, None])).astype(
        jnp.int32
    )
    left_pick = jnp.argmax(left_hits, axis=1)
    inner_index = jnp.take(left_cols, left_pick)
    right_hits = (
        right_live[None, :]
        & (right_rows[None, :] == inner_index[:, None])
        & (right_cols[None, :] == target_cols[:, None])
    ).astype(jnp.int32)
    right_pick = jnp.argmax(right_hits, axis=1)
    weight = (jnp.max(left_hits, axis=1) * jnp.max(right_hits, axis=1)).astype(jnp.float32)
    left_tiles = jnp.take(left_values, left_pick, axis=0)
    right_tiles = jnp.take(right_values, right_pick, axis=0)
    products = jnp.einsum(
        "opq,oqr->opr",
        left_tiles,
        right_tiles,
        precision=lax.Precision.HIGHEST,
        preferred_element_type=jnp.float32,
    )
    return running + products * weight[:, None, None]


def column_panel_of(listed):
    return flatten_list(lax.all_gather(listed, "row", axis=0, tiled=True))


def fold_over(column_panel, target_rows, target_cols, running, arrived):
    values, piece_rows, piece_cols, counts = arrived
    pieces_count = values.shape[1]
    tile_order = values.shape[-1]
    capacity = values.shape[-3]
    live_mask = live_slots(counts, capacity)
    shards = (
        values.reshape(pieces_count, -1, tile_order, tile_order),
        piece_rows.reshape(pieces_count, -1),
        piece_cols.reshape(pieces_count, -1),
        live_mask.reshape(pieces_count, -1),
    )

    def advance(carried, one_shard):
        return (tile_products(carried, one_shard, column_panel, target_rows, target_cols), None)

    running, unused = lax.scan(advance, running, shards)
    return running


def local(tile_values, tile_rows, tile_cols, tile_counts, out_rows, out_cols):
    tile_order = tile_values.shape[-1]
    own_list = (tile_values, tile_rows, tile_cols, tile_counts)
    column_panel = column_panel_of(own_list)
    layer_index = lax.axis_index("layer")
    target_rows = lax.dynamic_index_in_dim(out_rows[0, 0], layer_index, 0, keepdims=False)
    target_cols = lax.dynamic_index_in_dim(out_cols[0, 0], layer_index, 0, keepdims=False)
    empty_sums = jnp.zeros((target_rows.shape[0], tile_order, tile_order), jnp.float32)
    summed = fold_over(
        column_panel,
        target_rows,
        target_cols,
        empty_sums,
        (
            lax.all_gather(own_list[0], ("col", "layer"), axis=1, tiled=True),
            lax.all_gather(own_list[1], ("col", "layer"), axis=1, tiled=True),
            lax.all_gather(own_list[2], ("col", "layer"), axis=1, tiled=True),
            lax.all_gather(own_list[3], ("col", "layer"), axis=1, tiled=True),
        ),
    )
    result = summed.reshape(1, 1, -1, tile_order, tile_order)
    return result


def solution(mesh):
    in_specs = (
        P("row", ("col", "layer"), None, None, None, None),
        P("row", ("col", "layer"), None, None),
        P("row", ("col", "layer"), None, None),
        P("row", ("col", "layer"), None),
        P("row", "col", None, None),
        P("row", "col", None, None),
    )
    out_specs = P("row", ("col", "layer"), None, None, None)
    return jax.shard_map(local, mesh=mesh, in_specs=in_specs, out_specs=out_specs, check_vma=False)
```

profile of v0, /device:TPU:0, one launch (start us, length us, event | category | flops | bytes accessed | tf_op | source)
XLA Modules:
  0.0 310.3 jit_solution(2580711314461894590)
XLA Ops:
  8.0 2.1 all_gather.27
  10.1 2.0 all_gather.30
  12.0 2.0 all_gather.28
  14.2 42.4 %all_gather.24 = s32[1,16,2]{2,0,1:T(1,128)S(1)} all-gather(s32[1,1,2]{2,0,1:T(1,128)} %bitcast.55), channel_id=1, replica_groups=mesh['row'=2,'col'=8,'layer'=2] {'col','layer'}, dimensions={1}, use_global_device_ids=true | all-gather | bytes 136 | tf_op jit(solution)/shard_map/all_gather | solution.py:93
  57.0 36.1 %all_gather.25 = s32[1,16,2,6]{3,2,0,1:T(2,128)S(1)} all-gather(s32[1,1,2,6]{3,2,0,1:T(2,128)} %bitcast.52), channel_id=1, replica_groups=mesh['row'=2,'col'=8,'layer'=2] {'col','layer'}, dimensions={1}, use_global_device_ids=true | all-gather | bytes 816 | tf_op jit(solution)/shard_map/all_gather | solution.py:91
  93.2 38.3 %all_gather.29 = s32[1,16,2,6]{3,2,0,1:T(2,128)S(1)} all-gather(s32[1,1,2,6]{3,2,0,1:T(2,128)} %bitcast.53), channel_id=1, replica_groups=mesh['row'=2,'col'=8,'layer'=2] {'col','layer'}, dimensions={1}, use_global_device_ids=true | all-gather | bytes 816 | tf_op jit(solution)/shard_map/all_gather | solution.py:92
  132.3 45.5 %all-gather.3.cloned.1.call-done = f32[1,16,2,6,128,128]{5,4,3,2,0,1:T(8,128)} async-done(((f32[1,1,2,6,128,128]{5,4,3,2,0,1:T(8,128)}), f32[1,16,2,6,128,128]{5,4,3,2,0,1:T(8,128)}) %all-gather.3.cloned.1.call-update) | async-done | bytes 12582928 | tf_op jit(solution)/shard_map/all_gather | solution.py:90
  177.8 124.8 %while.12 = (s32[]{:T(128)}, f32[12,128,128]{2,1,0:T(8,128)S(1)}, pred[16,12]{1,0:T(8,128)(4,1)S(1)}, s32[16,12]{1,0:T(8,128)S(1)}, s32[12]{0:T(128)S(1)}, /*ind...) while((s32[]{:T(128)}, f32[12,128,128]{2,1,0:T(8,128)S(1)}, ...), condition=%wide.wide.region_5.6_spmd.clone, body=%wide.wide.region_0.5_spmd.clone.sunk | while | flops 302982272 | bytes 7875075 | solution.py:72
  180.2 2.0 gather_fusion.1
  182.6 1.2 dynamic-slice_bitcast_fusion.9
  184.4 1.1 fusion.22
  188.0 2.0 gather_fusion.1
  190.4 1.2 dynamic-slice_bitcast_fusion.9
  192.2 1.1 fusion.22
  195.8 2.0 gather_fusion.1
  198.2 1.2 dynamic-slice_bitcast_fusion.9
  200.1 1.1 fusion.22
  203.6 2.0 gather_fusion.1
  206.0 1.2 dynamic-slice_bitcast_fusion.9
  207.9 1.1 fusion.22
  211.4 2.0 gather_fusion.1
  213.8 1.2 dynamic-slice_bitcast_fusion.9
  215.7 1.1 fusion.22
  219.2 2.0 gather_fusion.1
  221.7 1.2 dynamic-slice_bitcast_fusion.9
  223.5 1.1 fusion.22
  227.0 2.0 gather_fusion.1
  229.5 1.2 dynamic-slice_bitcast_fusion.9
  231.3 1.1 fusion.22
  234.8 2.0 gather_fusion.1
  237.3 1.2 dynamic-slice_bitcast_fusion.9
  242.6 2.0 gather_fusion.1
  245.1 1.2 dynamic-slice_bitcast_fusion.9
  250.4 2.0 gather_fusion.1
  252.9 1.2 dynamic-slice_bitcast_fusion.9
  258.2 2.0 gather_fusion.1
  260.7 1.2 dynamic-slice_bitcast_fusion.9
  266.0 2.0 gather_fusion.1
  268.5 1.2 dynamic-slice_bitcast_fusion.9
  270.3 1.1 fusion.22
  273.9 2.0 gather_fusion.1
  276.3 1.2 dynamic-slice_bitcast_fusion.9
  281.7 2.0 gather_fusion.1
  284.1 1.2 dynamic-slice_bitcast_fusion.9
  289.5 2.0 gather_fusion.1
  291.9 1.2 dynamic-slice_bitcast_fusion.9
  297.3 2.0 gather_fusion.1
  299.7 1.2 dynamic-slice_bitcast_fusion.9
  (304 shorter events, 67.1 us)
Async XLA Ops:
  6.5 125.7 %all-gather.5.cloned.1.call-start = ((), (), s32[]{:S(2)}) async-start(), calls=%async_computation.1 | async-start | bytes 2359296 | tf_op jit(solution)/shard_map/all_gather | solution.py:53
  7.3 170.6 %all-gather.3.cloned.1.call-start = ((), (), s32[]{:S(2)}) async-start(), calls=%async_computation | async-start | bytes 13369344 | tf_op jit(solution)/shard_map/all_gather | solution.py:90
  12.0 165.8 %copy-start.1 = (s32[2,1,2,6]{3,2,1,0:T(2,128)}, s32[2,1,2,6]{3,2,1,0:T(2,128)S(1)}, u32[]{:S(2)}) copy-start(s32[2,1,2,6]{3,2,1,0:T(2,128)S(1)} %all_gather.30) | copy-start | bytes 292
  14.0 163.8 %copy-start.2 = (s32[2,1,2,6]{3,2,1,0:T(2,128)}, s32[2,1,2,6]{3,2,1,0:T(2,128)S(1)}, u32[]{:S(2)}) copy-start(s32[2,1,2,6]{3,2,1,0:T(2,128)S(1)} %all_gather.28) | copy-start | bytes 292
  302.6 0.9 copy-start
Sparse Core Ops, SparseCore 0:
  8.9 12.4 all-gather.4
  24.3 153.4 all-gather.2
where the time goes:
time: 312 us; the launch traced here: 310 us
  blocking collectives  123 us (39%)
  local copies, waits for them, and re-layouts  75.2 us (24%)
  waiting for transfers between devices  46.9 us (15%)
  other arithmetic  32.5 us (10%)
  matrix products  18.2 us (6%)
  between operations  13.4 us (4%)
    all_gather x1, waiting for transfers between devices, local(): lax.all_gather(own_list[0], ('col', 'layer'), axis=1, tiled=True)  45.5 us
    all_gather x1, blocking collectives, local(): lax.all_gather(own_list[3], ('col', 'layer'), axis=1, tiled=True)  42.4 us
    all_gather x1, blocking collectives, local(): lax.all_gather(own_list[2], ('col', 'layer'), axis=1, tiled=True)  38.3 us
    all_gather x1, blocking collectives, local(): lax.all_gather(own_list[1], ('col', 'layer'), axis=1, tiled=True)  36.1 us
    gather x16, local copies, waits for them, and re-layouts, tile_products(): right_tiles = jnp.take(right_values, right_pick, axis=0)  32.1 us
    squeeze x16, local copies, waits for them, and re-layouts, fold_over(): running, unused = lax.scan(advance, running, shards)  19.1 us
    dot_general x16, matrix products, tile_products(): jnp.einsum('opq,oqr->opr', left_tiles, right_tiles, precision=lax.Precisi...  18.2 us
    another operation x16, other arithmetic, tile_products(): right_pick = jnp.argmax(right_hits, axis=1)  12.3 us
  transfers between devices with their start and end apart: 2, of which 1 were waited for; matrix products, arithmetic and copies ran while one was open for 0% of the time, Pallas kernels for 0%

commit v1 on v0

v1 whole, which is shorter than its diff:
```python
import functools

import jax
import jax.numpy as jnp
from jax import lax
from jax.experimental import pallas as pl
from jax.experimental.pallas import tpu as pltpu
from jax.sharding import PartitionSpec as P

ROUND = 16
MESH = pl.DeviceIdType.MESH


def greet(others):
    barrier = pltpu.get_barrier_semaphore()
    count = len(others) if isinstance(others, list) else others[0]
    if isinstance(others, list):
        for device in others:
            pl.semaphore_signal(barrier, inc=1, device_id=device, device_id_type=MESH)
    else:
        make = others[1]

        def step(k, unused):
            pl.semaphore_signal(barrier, inc=1, device_id=make(k + 1), device_id_type=MESH)
            return unused

        lax.fori_loop(0, count, step, 0)
    pl.semaphore_wait(barrier, count)


def spread_kernel(
    n_row, n_sub, n_layer, tiles, meta, landed, panel, meta_all,
    send_sem, recv_sem, panel_send, panel_recv, meta_send, meta_recv, local_sem,
):
    row = lax.axis_index("row")
    sub = lax.axis_index("col") * n_layer + lax.axis_index("layer")
    total = n_row * n_sub
    flat = row * n_sub + sub

    def device_at(flat_index):
        band, place = flat_index // n_sub, flat_index % n_sub
        return {"row": band, "col": place // n_layer, "layer": place % n_layer}

    def other(k):
        return device_at(lax.rem(flat + k, total))

    greet((total - 1, other))

    def meta_copy(k):
        return pltpu.make_async_remote_copy(
            src_ref=meta, dst_ref=meta_all.at[flat], send_sem=meta_send.at[k],
            recv_sem=meta_recv.at[k], device_id=other(k), device_id_type=MESH)

    def slice_copy(k):
        place = lax.rem(sub + k, n_sub)
        return pltpu.make_async_remote_copy(
            src_ref=tiles.at[:, place], dst_ref=landed.at[sub], send_sem=send_sem.at[k],
            recv_sem=recv_sem.at[k],
            device_id={"row": row, "col": place // n_layer, "layer": place % n_layer},
            device_id_type=MESH)

    def panel_copy(k):
        return pltpu.make_async_remote_copy(
            src_ref=tiles, dst_ref=panel.at[row], send_sem=panel_send.at[k],
            recv_sem=panel_recv.at[k],
            device_id={"row": lax.rem(row + k, n_row), "col": sub // n_layer,
                       "layer": sub % n_layer},
            device_id_type=MESH)

    def each(count, what):
        def step(k, unused):
            what(k + 1)
            return unused
        lax.fori_loop(0, count, step, 0)

    own_meta = pltpu.make_async_copy(meta, meta_all.at[flat], local_sem.at[0])
    own_slice = pltpu.make_async_copy(tiles.at[:, sub], landed.at[sub], local_sem.at[1])
    own_panel = pltpu.make_async_copy(tiles, panel.at[row], local_sem.at[2])
    each(total - 1, lambda k: meta_copy(k).start())
    each(n_sub - 1, lambda k: slice_copy(k).start())
    each(n_row - 1, lambda k: panel_copy(k).start())
    own_meta.start()
    own_slice.start()
    own_panel.start()
    own_meta.wait()
    own_slice.wait()
    own_panel.wait()
    each(total - 1, lambda k: meta_copy(k).wait())
    each(n_row - 1, lambda k: panel_copy(k).wait())
    each(n_sub - 1, lambda k: slice_copy(k).wait())


def deliver_kernel(n_sub, n_layer, wanted, landed, arrived, packed, send_sem, recv_sem, local_sem):
    row = lax.axis_index("row")
    sub = lax.axis_index("col") * n_layer + lax.axis_index("layer")

    def device_of(place):
        return {"row": row, "col": place // n_layer, "layer": place % n_layer}

    greet((n_sub - 1, lambda k: device_of(lax.rem(sub + k, n_sub))))

    def pack(place):
        for n in range(ROUND):
            packed[place, n] = landed[wanted[place, n]]

    def send(k):
        place = lax.rem(sub + k, n_sub)
        return pltpu.make_async_remote_copy(
            src_ref=packed.at[place], dst_ref=arrived.at[:, sub], send_sem=send_sem.at[k],
            recv_sem=recv_sem.at[k], device_id=device_of(place), device_id_type=MESH)

    def out_step(k, unused):
        pack(lax.rem(sub + k + 1, n_sub))
        send(k + 1).start()
        return unused

    def wait_step(k, unused):
        send(k + 1).wait()
        return unused

    lax.fori_loop(0, n_sub - 1, out_step, 0)
    pack(sub)
    own = pltpu.make_async_copy(packed.at[sub], arrived.at[:, sub], local_sem)
    own.start()
    own.wait()
    lax.fori_loop(0, n_sub - 1, wait_step, 0)


def multiply_kernel(base, counts, listed, arrived, panel, out):
    order = out.shape[-1]

    def split(value):
        high = value.astype(jnp.bfloat16)
        return high, (value - high.astype(jnp.float32)).astype(jnp.bfloat16)

    def product(left, right):
        left_high, left_low = split(left)
        right_high, right_low = split(right)
        lefts = jnp.concatenate([left_high, left_high, left_low], axis=1)
        rights = jnp.concatenate([right_high, right_low, right_high], axis=0)
        return jnp.dot(lefts, rights, preferred_element_type=jnp.float32)

    for o in range(out.shape[0]):
        def add(m, unused):
            code = listed[o, m]
            left_index = code // base
            right = panel[code % base]

            @pl.when(left_index < ROUND)
            def _():
                out[o] += product(arrived[left_index], right)

            @pl.when(left_index >= ROUND)
            def _():
                out[o] += product(panel[left_index - ROUND], right)

            return unused

        out[o] = jnp.zeros((order, order), jnp.float32)
        lax.fori_loop(0, counts[o], add, 0)


def running_count(flags):
    size = flags.shape[-1]
    upper = (jnp.arange(size)[:, None] <= jnp.arange(size)[None, :]).astype(jnp.bfloat16)
    return jnp.dot(flags.astype(jnp.bfloat16), upper,
                   preferred_element_type=jnp.float32).astype(jnp.int32)


def local(n_row, n_col, n_layer, tile_values, tile_rows, tile_cols, tile_counts, out_rows, out_cols):
    order = tile_values.shape[-1]
    slots = tile_values.shape[2] * tile_values.shape[3]
    kept = out_rows.shape[-1]
    n_sub = n_col * n_layer
    part = order // n_sub
    total = n_row * n_sub
    row = lax.axis_index("row")
    layer = lax.axis_index("layer")
    sub = lax.axis_index("col") * n_layer + layer

    tiles = tile_values.reshape(slots, n_sub, part, order)
    live = jnp.arange(tile_rows.shape[-1]) < tile_counts[0, 0][:, None]
    own_rows = jnp.where(live, tile_rows[0, 0], -1).reshape(-1)
    own_cols = tile_cols.reshape(-1)
    target_rows = lax.dynamic_index_in_dim(out_rows[0, 0], layer, 0, keepdims=False)
    target_cols = lax.dynamic_index_in_dim(out_cols[0, 0], layer, 0, keepdims=False)
    pieces = jnp.concatenate([own_rows, own_cols, target_rows, target_cols])
    meta = jnp.zeros((8, 128), jnp.int32).at[0, : pieces.shape[0]].set(pieces)

    anywhere = pl.BlockSpec(memory_space=pl.ANY)
    landed, panel, meta_all = pl.pallas_call(
        functools.partial(spread_kernel, n_row, n_sub, n_layer),
        out_shape=(
            jax.ShapeDtypeStruct((n_sub, slots, part, order), jnp.float32),
            jax.ShapeDtypeStruct((n_row, slots, n_sub, part, order), jnp.float32),
            jax.ShapeDtypeStruct((total, 8, 128), jnp.int32),
        ),
        in_specs=[anywhere, anywhere],
        out_specs=(anywhere, anywhere, anywhere),
        scratch_shapes=[
            pltpu.SemaphoreType.DMA((n_sub,)),
            pltpu.SemaphoreType.DMA((n_sub,)),
            pltpu.SemaphoreType.DMA((n_row,)),
            pltpu.SemaphoreType.DMA((n_row,)),
            pltpu.SemaphoreType.DMA((total,)),
            pltpu.SemaphoreType.DMA((total,)),
            pltpu.SemaphoreType.DMA((3,)),
        ],
        compiler_params=pltpu.CompilerParams(collective_id=1, has_side_effects=True),
        name="spread",
    )(tiles, meta)
    landed = landed.reshape(n_sub * slots, part, order)
    panel = panel.reshape(n_row * slots, order, order)

    lines = meta_all[:, 0, : 2 * slots + 2 * kept].reshape(n_row, n_sub, -1)
    list_rows = lines[:, :, :slots]
    list_cols = lines[:, :, slots : 2 * slots]
    goal_rows = lines[:, :, 2 * slots : 2 * slots + kept]
    goal_cols = lines[:, :, 2 * slots + kept :]
    bits = jnp.left_shift(1, jnp.arange(kept, dtype=jnp.int32))
    left_rows = list_rows.reshape(n_row, n_sub * slots)
    left_cols = list_cols.reshape(n_row, n_sub * slots)
    right_rows = list_rows.transpose(1, 0, 2).reshape(n_sub, n_row * slots)
    right_cols = list_cols.transpose(1, 0, 2).reshape(n_sub, n_row * slots)
    left_bits = jnp.sum(jnp.where(
        left_rows[:, None, None, :] == goal_rows[:, :, :, None], bits[:, None], 0), axis=2)
    right_bits = jnp.sum(jnp.where(
        right_cols[None, :, :, None] == goal_cols[:, :, None, :], bits, 0), axis=3)
    meets = (
        (right_rows[None, :, :, None] == left_cols[:, None, None, :])
        & (jnp.bitwise_and(left_bits[:, :, None, :], right_bits[:, :, :, None]) != 0)
    )
    away = (jnp.arange(n_sub * slots) // slots)[None, :] != jnp.arange(n_sub)[:, None]
    needed = jnp.any(meets, axis=2) & away
    most = jnp.max(jnp.sum(needed.astype(jnp.int32), axis=-1))
    rounds = (most + ROUND - 1) // ROUND
    my_needed = lax.dynamic_index_in_dim(needed, row, 0, keepdims=False)
    rank = jnp.where(my_needed, running_count(my_needed) - 1, -1)
    slot_ids = jnp.arange(n_sub * slots, dtype=jnp.int32)

    my_left_rows = lax.dynamic_index_in_dim(left_rows, row, 0, keepdims=False)
    my_left_cols = lax.dynamic_index_in_dim(left_cols, row, 0, keepdims=False)
    my_goal_rows, my_goal_cols = target_rows, target_cols
    my_right_rows = lax.dynamic_index_in_dim(right_rows, sub, 0, keepdims=False)
    my_right_cols = lax.dynamic_index_in_dim(right_cols, sub, 0, keepdims=False)
    base = n_row * slots

    def one_round(turn, collective_id):
        places = turn * ROUND + jnp.arange(ROUND, dtype=jnp.int32)
        chosen = rank[:, None, :] == places[None, :, None]
        wanted = jnp.sum(jnp.where(chosen, slot_ids, 0), axis=-1)
        arrived = pl.pallas_call(
            functools.partial(deliver_kernel, n_sub, n_layer),
            out_shape=jax.ShapeDtypeStruct((ROUND, n_sub, part, order), jnp.float32),
            in_specs=[
                pl.BlockSpec(memory_space=pltpu.SMEM),
                pl.BlockSpec(memory_space=pltpu.VMEM),
            ],
            out_specs=anywhere,
            scratch_shapes=[
                pltpu.VMEM((n_sub, ROUND, part, order), jnp.float32),
                pltpu.SemaphoreType.DMA((n_sub,)),
                pltpu.SemaphoreType.DMA((n_sub,)),
                pltpu.SemaphoreType.DMA,
            ],
            compiler_params=pltpu.CompilerParams(
                collective_id=collective_id, has_side_effects=True,
                vmem_limit_bytes=32 * 1024 * 1024),
            name="deliver",
        )(wanted, landed)
        arrived = arrived.reshape(ROUND, order, order)

        my_chosen = lax.dynamic_index_in_dim(chosen, sub, 0, keepdims=False)
        far_rows = jnp.max(jnp.where(my_chosen, my_left_rows, -1), axis=-1)
        far_cols = jnp.max(jnp.where(my_chosen, my_left_cols, -1), axis=-1)
        near_rows = jnp.where(turn == 0, own_rows, -1)
        rows = jnp.concatenate([far_rows, near_rows])
        cols = jnp.concatenate([far_cols, own_cols])
        names = jnp.concatenate([
            jnp.arange(ROUND, dtype=jnp.int32),
            ROUND + row * slots + jnp.arange(slots, dtype=jnp.int32)])
        hits = (
            (rows[None, :, None] == my_goal_rows[:, None, None]) & (rows[None, :, None] >= 0)
            & (cols[None, :, None] == my_right_rows[None, None, :])
            & (my_right_cols[None, None, :] == my_goal_cols[:, None, None])
        )
        partner = jnp.max(
            jnp.where(hits, jnp.arange(base, dtype=jnp.int32), -1), axis=-1)
        flags = partner >= 0
        place = jnp.where(flags, running_count(flags) - 1, -1)
        counts = jnp.sum(flags.astype(jnp.int32), axis=-1)
        codes = names[None, :] * base + partner
        at_place = place[:, None, :] == jnp.arange(n_sub, dtype=jnp.int32)[None, :, None]
        listed = jnp.sum(jnp.where(at_place, codes[:, None, :], 0), axis=-1)
        return pl.pallas_call(
            functools.partial(multiply_kernel, base),
            out_shape=jax.ShapeDtypeStruct((kept, order, order), jnp.float32),
            in_specs=[
                pl.BlockSpec(memory_space=pltpu.SMEM),
                pl.BlockSpec(memory_space=pltpu.SMEM),
                pl.BlockSpec(memory_space=pltpu.VMEM),
                pl.BlockSpec(memory_space=pltpu.VMEM),
            ],
            out_specs=pl.BlockSpec(memory_space=pltpu.VMEM),
            compiler_params=pltpu.CompilerParams(vmem_limit_bytes=32 * 1024 * 1024),
            name="multiply",
        )(counts, listed, arrived, panel)

    summed = one_round(0, 2)

    def more(state):
        turn, unused = state
        return turn < rounds

    def again(state):
        turn, so_far = state
        return turn + 1, so_far + one_round(turn, 3)

    unused, summed = lax.while_loop(more, again, (jnp.int32(1), summed))
    return summed.reshape(1, 1, kept, order, order)


def solution(mesh):
    in_specs = (
        P("row", ("col", "layer"), None, None, None, None),
        P("row", ("col", "layer"), None, None),
        P("row", ("col", "layer"), None, None),
        P("row", ("col", "layer"), None),
        P("row", "col", None, None),
        P("row", "col", None, None),
    )
    out_specs = P("row", ("col", "layer"), None, None, None)
    body = functools.partial(local, mesh.shape["row"], mesh.shape["col"], mesh.shape["layer"])
    return jax.shard_map(body, mesh=mesh, in_specs=in_specs, out_specs=out_specs, check_vma=False)
```

time: 312 us -> 69.4 us (0.22)
  the two profiles are of different devices: /device:TPU:0 before, /device:TPU:14 now
where the time goes in v1:
time: 69.4 us; the launch traced here: 68.9 us
  Pallas kernels  58.8 us (85%)
  local copies, waits for them, and re-layouts  5.33 us (8%)
  other arithmetic  3.65 us (5%)
  between operations  0.81 us (1%)
    pallas_call x1, Pallas kernels, one_round(): pl.pallas_call(functools.partial(deliver_kernel, n_sub, n_layer), out_sha...  29.2 us
    pallas_call x1, Pallas kernels, local(): pl.pallas_call(functools.partial(spread_kernel, n_row, n_sub, n_layer), o...  26.9 us
    pallas_call x1, Pallas kernels, one_round(): pl.pallas_call(functools.partial(multiply_kernel, base), out_shape=jax.Sh...  2.69 us

profile of v1, /device:TPU:14, one launch (start us, length us, event | category | flops | bytes accessed | tf_op | source)
XLA Modules:
  0.0 68.9 jit_solution(3046577423001850194)
XLA Ops:
  0.0 0.0 copy-start
  0.0 0.8 %reshape.438 = s32[12]{0:T(128)S(1)} reshape(s32[1,1,2,6]{3,2,1,0:T(2,128)} %param.12) | data formatting | bytes 96 | tf_op jit(solution)/shard_map/reshape | solution.py:184
  0.8 0.0 copy-done
  0.8 0.7 fusion.15
  1.5 0.8 %squeeze.37 = s32[12]{0:T(128)S(1)} reshape(s32[1,1,2,6]{3,2,1,0:T(2,128)} %param.11) | data formatting | bytes 96 | tf_op jit(solution)/shard_map/squeeze | solution.py:183
  2.2 0.7 %iota_compare_fusion.10 = pred[2,6]{1,0:T(4,128)(4,1)S(1)} fusion(s32[2]{0:T(128)} %bitcast.55), kind=kLoop, calls=%fused_computation.69 | loop fusion | flops 12 | bytes 20 | tf_op jit(solution)/shard_map/lt | solution.py:182
  3.0 0.1 lt.53
  3.1 0.1 add_bitcast_fusion
  3.2 0.6 scatter.4.meta
  3.8 26.9 %spread.1 = (f32[16,12,8,128]{3,2,1,0:T(8,128)S(1)}, f32[2,12,16,8,128]{4,3,2,1,0:T(8,128)S(1)}, s32[32,8,128]{2,1,0:T(8,128)}) custom-call(f32[12,16,8,128]{3,2,1,0:T(8,128)} %bitcast.48, s32[8,128]{1,0:T(8,128)} %scatter.4.meta), custom_call_target="tpu_custom_call" | custom-call | tf_op jit(solution)/shard_map/spread/pallas_call | solution.py:191
  30.7 0.9 %slice.31 = s32[32,1,48]{2,1,0:T(1,128)S(1)} slice(s32[32,8,128]{2,1,0:T(8,128)} %get-tuple-element.237), slice={[0:32], [0:1], [0:48]} | slice | bytes 12288 | tf_op jit(solution)/shard_map/slice | solution.py:215
  31.6 0.1 slice_bitcast_fusion
  31.7 0.1 eq.240
  31.8 0.1 eq.245
  31.9 0.1 eq.242
  32.0 0.1 eq.249
  32.1 0.1 broadcast_compare_fusion.7
  32.2 0.1 copy.16
  32.3 0.1 select_reduce_fusion.6
  32.4 0.1 copy.15
  32.5 0.1 select_reduce_fusion.4
  32.6 0.4 fusion.10
  33.0 0.1 convert_reduce_fusion.1
  33.1 0.6 reduce_max.75
  34.4 0.1 fusion.6
  34.6 0.4 select_reduce_fusion.5.wanted
  35.0 0.1 select_reduce_fusion.10
  35.1 0.1 pad_add_fusion.3
  35.2 0.1 broadcast_compare_fusion.8
  35.3 0.1 compare_and_fusion.1
  35.3 0.1 broadcast_compare_fusion.5
  35.4 0.1 select_reduce_fusion.7
  35.6 0.1 convert_reduce_fusion.2
  35.7 0.1 fusion.8
  35.8 0.3 select_reduce_fusion.8.listed
  36.1 29.2 %deliver.5 = f32[16,16,8,128]{3,2,1,0:T(8,128)S(1)} custom-call(s32[16,16]{1,0:T(8,128)S(1)} %select_reduce_fusion.5.wanted, f32[192,8,128]{2,1,0:T(8,128)S(1)} %bitcast.46), custom_call_target="tpu_custom_call" | custom-call | tf_op jit(solution)/shard_map/deliver/pallas_call | solution.py:252
  65.3 2.7 %multiply.5 = f32[12,128,128]{2,1,0:T(8,128)S(1)} custom-call(s32[12]{0:T(128)S(1)} %get-tuple-element.318.counts, s32[12,16]{1,0:T(8,128)S(1)} %select_reduce_fusion.8.listed, f32[16,128,128]{2,1,0:T(8,128)S(1)} %bitcast.43, f32[24,128,128]{2,1,0:T(8,128)S(1)} %bitcast.44), custom_call_target="tpu_custom_call" | custom-call | tf_op jit(solution)/shard_map/multiply/pallas_call | solution.py:295
  68.0 0.0 copy-start.1
  68.0 0.9 %copy-done.1 = f32[12,128,128]{2,1,0:T(8,128)} copy-done((f32[12,128,128]{2,1,0:T(8,128)}, f32[12,128,128]{2,1,0:T(8,128)S(1)}, u32[]{:S(2)}) %copy-start.1) | copy-done | bytes 786456
  (14 shorter events, 0.1 us)
Async XLA Ops:
  0.0 0.8 %copy-start = (s32[1,1,2,12]{3,2,1,0:T(2,128)S(1)}, s32[1,1,2,12]{3,2,1,0:T(2,128)}, u32[]{:S(2)}) copy-start(s32[1,1,2,12]{3,2,1,0:T(2,128)} %param.14) | copy-start | bytes 292
  68.0 0.9 %copy-start.1 = (f32[12,128,128]{2,1,0:T(8,128)}, f32[12,128,128]{2,1,0:T(8,128)S(1)}, u32[]{:S(2)}) copy-start(f32[12,128,128]{2,1,0:T(8,128)S(1)} %get-tuple-element.240) | copy-start | bytes 2359300

commit v2 on v1

--- a/solution.py
+++ b/solution.py
@@ -7,30 +7,28 @@
 from jax.experimental.pallas import tpu as pltpu
 from jax.sharding import PartitionSpec as P
 
-ROUND = 16
+ROUND = 14
 MESH = pl.DeviceIdType.MESH
 
 
-def greet(others):
+def greet(count, device_of):
     barrier = pltpu.get_barrier_semaphore()
-    count = len(others) if isinstance(others, list) else others[0]
-    if isinstance(others, list):
-        for device in others:
-            pl.semaphore_signal(barrier, inc=1, device_id=device, device_id_type=MESH)
-    else:
-        make = others[1]
-
-        def step(k, unused):
-            pl.semaphore_signal(barrier, inc=1, device_id=make(k + 1), device_id_type=MESH)
-            return unused
-
-        lax.fori_loop(0, count, step, 0)
+
+    def step(k, unused):
+        pl.semaphore_signal(barrier, inc=1, device_id=device_of(k + 1), device_id_type=MESH)
+        return unused
+
+    lax.fori_loop(0, count, step, 0)
     pl.semaphore_wait(barrier, count)
 
 
+def far_first(k, n_sub):
+    return n_sub // 2 + (1 - 2 * ((k + 1) % 2)) * ((k + 1) // 2)
+
+
 def spread_kernel(
-    n_row, n_sub, n_layer, tiles, meta, landed, panel, meta_all,
-    send_sem, recv_sem, panel_send, panel_recv, meta_send, meta_recv, local_sem,
+    n_row, n_sub, n_layer, tiles, rows, cols, counts, goal_rows, goal_cols, landed, panel, meta_all,
+    meta, send_sem, recv_sem, panel_send, panel_recv, meta_send, meta_recv, local_sem,
 ):
     row = lax.axis_index("row")
     sub = lax.axis_index("col") * n_layer + lax.axis_index("layer")
@@ -44,7 +42,16 @@
     def other(k):
         return device_at(lax.rem(flat + k, total))
 
-    greet((total - 1, other))
+    greet(total - 1, other)
+
+    lists, slots = rows.shape
+    layers, kept = goal_rows.shape
+    meta[...] = jnp.zeros_like(meta)
+    live = lax.broadcasted_iota(jnp.int32, (lists, slots), 1) < counts[...]
+    meta[0:lists, 0:slots] = jnp.where(live, rows[...], -1)
+    meta[lists : 2 * lists, 0:slots] = cols[...]
+    meta[2 * lists : 2 * lists + layers, 0:kept] = goal_rows[...]
+    meta[2 * lists + layers : 2 * lists + 2 * layers, 0:kept] = goal_cols[...]
 
     def meta_copy(k):
         return pltpu.make_async_remote_copy(
@@ -76,8 +83,8 @@
     own_meta = pltpu.make_async_copy(meta, meta_all.at[flat], local_sem.at[0])
     own_slice = pltpu.make_async_copy(tiles.at[:, sub], landed.at[sub], local_sem.at[1])
     own_panel = pltpu.make_async_copy(tiles, panel.at[row], local_sem.at[2])
+    each(n_sub - 1, lambda k: slice_copy(far_first(k - 1, n_sub)).start())
     each(total - 1, lambda k: meta_copy(k).start())
-    each(n_sub - 1, lambda k: slice_copy(k).start())
     each(n_row - 1, lambda k: panel_copy(k).start())
     own_meta.start()
     own_slice.start()
@@ -97,7 +104,7 @@
     def device_of(place):
         return {"row": row, "col": place // n_layer, "layer": place % n_layer}
 
-    greet((n_sub - 1, lambda k: device_of(lax.rem(sub + k, n_sub))))
+    greet(n_sub - 1, lambda k: device_of(lax.rem(sub + k, n_sub)))
 
     def pack(place):
         for n in range(ROUND):
@@ -110,8 +117,9 @@
             recv_sem=recv_sem.at[k], device_id=device_of(place), device_id_type=MESH)
 
     def out_step(k, unused):
-        pack(lax.rem(sub + k + 1, n_sub))
-        send(k + 1).start()
+        shift = far_first(k, n_sub)
+        pack(lax.rem(sub + shift, n_sub))
+        send(shift).start()
         return unused
 
     def wait_step(k, unused):
@@ -179,13 +187,8 @@
     sub = lax.axis_index("col") * n_layer + layer
 
     tiles = tile_values.reshape(slots, n_sub, part, order)
-    live = jnp.arange(tile_rows.shape[-1]) < tile_counts[0, 0][:, None]
-    own_rows = jnp.where(live, tile_rows[0, 0], -1).reshape(-1)
     own_cols = tile_cols.reshape(-1)
-    target_rows = lax.dynamic_index_in_dim(out_rows[0, 0], layer, 0, keepdims=False)
-    target_cols = lax.dynamic_index_in_dim(out_cols[0, 0], layer, 0, keepdims=False)
-    pieces = jnp.concatenate([own_rows, own_cols, target_rows, target_cols])
-    meta = jnp.zeros((8, 128), jnp.int32).at[0, : pieces.shape[0]].set(pieces)
+    lists = tile_rows.shape[2]
 
     anywhere = pl.BlockSpec(memory_space=pl.ANY)
     landed, panel, meta_all = pl.pallas_call(
@@ -195,9 +198,10 @@
             jax.ShapeDtypeStruct((n_row, slots, n_sub, part, order), jnp.float32),
             jax.ShapeDtypeStruct((total, 8, 128), jnp.int32),
         ),
-        in_specs=[anywhere, anywhere],
+        in_specs=[anywhere] + [pl.BlockSpec(memory_space=pltpu.VMEM)] * 5,
         out_specs=(anywhere, anywhere, anywhere),
         scratch_shapes=[
+            pltpu.VMEM((8, 128), jnp.int32),
             pltpu.SemaphoreType.DMA((n_sub,)),
             pltpu.SemaphoreType.DMA((n_sub,)),
             pltpu.SemaphoreType.DMA((n_row,)),
@@ -208,15 +212,22 @@
         ],
         compiler_params=pltpu.CompilerParams(collective_id=1, has_side_effects=True),
         name="spread",
-    )(tiles, meta)
+    )(tiles, tile_rows[0, 0], tile_cols[0, 0], tile_counts.reshape(lists, 1),
+      out_rows[0, 0], out_cols[0, 0])
     landed = landed.reshape(n_sub * slots, part, order)
     panel = panel.reshape(n_row * slots, order, order)
 
-    lines = meta_all[:, 0, : 2 * slots + 2 * kept].reshape(n_row, n_sub, -1)
-    list_rows = lines[:, :, :slots]
-    list_cols = lines[:, :, slots : 2 * slots]
-    goal_rows = lines[:, :, 2 * slots : 2 * slots + kept]
-    goal_cols = lines[:, :, 2 * slots + kept :]
+    lines = meta_all.reshape(n_row, n_col, n_layer, 8, 128)
+    per_list = slots // lists
+    list_rows = lines[..., 0:lists, :per_list].reshape(n_row, n_sub, slots)
+    list_cols = lines[..., lists : 2 * lists, :per_list].reshape(n_row, n_sub, slots)
+    goals = lines[:, :, 0, 2 * lists : 2 * lists + 2 * n_layer, :kept]
+    goal_rows = goals[:, :, :n_layer].reshape(n_row, n_sub, kept)
+    goal_cols = goals[:, :, n_layer:].reshape(n_row, n_sub, kept)
+    live = jnp.arange(per_list) < tile_counts[0, 0][:, None]
+    own_rows = jnp.where(live, tile_rows[0, 0], -1).reshape(-1)
+    target_rows = lax.dynamic_index_in_dim(out_rows[0, 0], layer, 0, keepdims=False)
+    target_cols = lax.dynamic_index_in_dim(out_cols[0, 0], layer, 0, keepdims=False)
     bits = jnp.left_shift(1, jnp.arange(kept, dtype=jnp.int32))
     left_rows = list_rows.reshape(n_row, n_sub * slots)
     left_cols = list_cols.reshape(n_row, n_sub * slots)
@@ -245,7 +256,7 @@
     my_right_cols = lax.dynamic_index_in_dim(right_cols, sub, 0, keepdims=False)
     base = n_row * slots
 
-    def one_round(turn, collective_id):
+    def deliver(turn, collective_id):
         places = turn * ROUND + jnp.arange(ROUND, dtype=jnp.int32)
         chosen = rank[:, None, :] == places[None, :, None]
         wanted = jnp.sum(jnp.where(chosen, slot_ids, 0), axis=-1)
@@ -265,11 +276,12 @@
             ],
             compiler_params=pltpu.CompilerParams(
                 collective_id=collective_id, has_side_effects=True,
-                vmem_limit_bytes=32 * 1024 * 1024),
+                vmem_limit_bytes=16 * 1024 * 1024),
             name="deliver",
         )(wanted, landed)
-        arrived = arrived.reshape(ROUND, order, order)
-
+        return arrived.reshape(ROUND, order, order), chosen
+
+    def products(turn, arrived, chosen):
         my_chosen = lax.dynamic_index_in_dim(chosen, sub, 0, keepdims=False)
         far_rows = jnp.max(jnp.where(my_chosen, my_left_rows, -1), axis=-1)
         far_cols = jnp.max(jnp.where(my_chosen, my_left_cols, -1), axis=-1)
@@ -302,21 +314,21 @@
                 pl.BlockSpec(memory_space=pltpu.VMEM),
             ],
             out_specs=pl.BlockSpec(memory_space=pltpu.VMEM),
-            compiler_params=pltpu.CompilerParams(vmem_limit_bytes=32 * 1024 * 1024),
+            compiler_params=pltpu.CompilerParams(vmem_limit_bytes=16 * 1024 * 1024),
             name="multiply",
         )(counts, listed, arrived, panel)
 
-    summed = one_round(0, 2)
-
-    def more(state):
-        turn, unused = state
-        return turn < rounds
-
-    def again(state):
-        turn, so_far = state
-        return turn + 1, so_far + one_round(turn, 3)
-
-    unused, summed = lax.while_loop(more, again, (jnp.int32(1), summed))
+    arrived, chosen = deliver(0, 2)
+
+    def more_rounds():
+        def again(state):
+            turn, so_far = state
+            return turn + 1, so_far + products(turn, *deliver(turn, 3))
+
+        start = (jnp.int32(1), products(0, arrived, chosen))
+        return lax.while_loop(lambda state: state[0] < rounds, again, start)[1]
+
+    summed = lax.cond(rounds > 1, more_rounds, lambda: products(0, arrived, chosen))
     return summed.reshape(1, 1, kept, order, order)
 
 

time: 69.4 us -> 70.3 us (1.013)
  the two profiles are of different devices: /device:TPU:14 before, /device:TPU:0 now
where the time goes in v2:
time: 70.3 us; the launch traced here: 69.8 us
  Pallas kernels  58.8 us (84%)
  local copies, waits for them, and re-layouts  6.25 us (9%)
  other arithmetic  3.65 us (5%)
  between operations  0.78 us (1%)
    pallas_call x1, Pallas kernels, local(): pl.pallas_call(functools.partial(spread_kernel, n_row, n_sub, n_layer), o...  29.9 us
    pallas_call x1, Pallas kernels, deliver(): pl.pallas_call(functools.partial(deliver_kernel, n_sub, n_layer), out_sha...  25.9 us
    pallas_call x1, Pallas kernels, products(): pl.pallas_call(functools.partial(multiply_kernel, base), out_shape=jax.Sh...  2.99 us

profile of v2, /device:TPU:0, one launch (start us, length us, event | category | flops | bytes accessed | tf_op | source)
XLA Modules:
  0.0 69.8 jit_solution(1312654268527142252)
XLA Ops:
  0.0 0.8 %reshape.559 = s32[12]{0:T(128)S(1)} reshape(s32[1,1,2,6]{3,2,1,0:T(2,128)} %param.12) | data formatting | bytes 96 | tf_op jit(solution)/shard_map/reshape | solution.py:190
  0.8 0.7 %iota_compare_fusion.13 = pred[2,6]{1,0:T(4,128)(4,1)S(1)} fusion(s32[2]{0:T(128)} %bitcast.73), kind=kLoop, calls=%fused_computation.92 | loop fusion | flops 12 | bytes 20 | tf_op jit(solution)/shard_map/lt | solution.py:227
  1.5 0.1 lt.57
  1.6 0.8 %squeeze.66 = s32[12]{0:T(128)S(1)} reshape(s32[1,1,2,6]{3,2,1,0:T(2,128)} %param.11) | data formatting | bytes 96 | tf_op jit(solution)/shard_map/squeeze | solution.py:215
  2.3 0.7 %fusion.13 = (s32[12]{0:T(128)S(1)}, s32[12]{0:T(128)S(1)}) fusion(s32[1,1,2,12]{3,2,1,0:T(2,128)} %param.15, s32[]{:T(128)S(6)} %select_n.169, s32[1,1,2,12]{3,2,1,0:T(2,128)} %param.14), kind=kLoop, calls=%fused_computation.93 | loop fusion | bytes 196 | tf_op jit(solution)/shard_map/jit(dynamic_index_in_dim)/squeeze | solution.py:230
  3.0 1.3 %copy.23.counts = s32[2,1]{1,0:T(2,128)} copy(s32[2,1]{0,1:T(1,128)} %bitcast.74) | data formatting | bytes 16 | tf_op jit(solution)/shard_map/reshape | solution.py:215
  4.4 29.9 %spread.1 = (f32[16,12,8,128]{3,2,1,0:T(8,128)S(1)}, f32[2,12,16,8,128]{4,3,2,1,0:T(8,128)S(1)}, s32[32,8,128]{2,1,0:T(8,128)}) custom-call(f32[12,16,8,128]{3,2,1,0:T(8,128)} %bitcast.58, s32[2,6]{1,0:T(2,128)} %bitcast.71, s32[2,6]{1,0:T(2,128)} %bitcast.72, s32[2,1]{1,0:T(2,128)} %copy.23.counts, s32[2,12]{1,0:T(2,128)} %bitcast.69, s32[2,12]{1,0:T(2,128)} %bitcast.70), custom_call_target="tpu_custom_call" | custom-call | tf_op jit(solution)/shard_map/spread/pallas_call | solution.py:194
  34.3 0.8 %slice_bitcast_fusion = s32[2,8,4,12]{3,2,1,0:T(4,128)S(1)} fusion(s32[2,8,2,8,128]{4,3,2,1,0:T(8,128)} %bitcast.59), kind=kLoop, calls=%fused_computation.75 | loop fusion | bytes 6144 | tf_op jit(solution)/shard_map/squeeze | solution.py:224
  35.2 1.0 %fusion.17 = (s32[2,8,2,2,6]{4,3,2,1,0:T(2,128)S(1)}, s32[2,8,2,2,6]{4,3,2,1,0:T(2,128)S(1)}) fusion(s32[2,8,2,8,128]{4,3,2,1,0:T(8,128)} %bitcast.60), kind=kLoop, calls=%fused_computation.99 | loop fusion | bytes 6144 | tf_op jit(solution)/shard_map/slice | solution.py:222
  36.2 0.1 copy.25
  36.3 0.1 copy.27
  36.4 0.1 eq.314
  36.5 0.1 reshape.557
  36.6 0.1 eq.309
  36.7 0.1 eq.311
  36.8 0.1 reshape.558
  36.9 0.1 eq.319
  37.0 0.1 select_reduce_fusion.15
  37.2 0.1 select_reduce_fusion.13
  37.3 0.4 fusion.9
  37.7 0.1 convert_reduce_fusion.3
  37.8 0.6 reduce_max.99
  39.1 0.1 fusion.7
  39.2 0.4 select_reduce_fusion.14.wanted
  39.7 25.9 %deliver.5 = f32[14,16,8,128]{3,2,1,0:T(8,128)S(1)} custom-call(s32[16,14]{1,0:T(8,128)S(1)} %select_reduce_fusion.14.wanted, f32[192,8,128]{2,1,0:T(8,128)S(1)} %bitcast.54), custom_call_target="tpu_custom_call" | custom-call | tf_op jit(solution)/shard_map/deliver/pallas_call | solution.py:263
  65.5 4.3 %conditional.1 = (f32[1,1,12,128,128]{4,3,2,1,0:T(8,128)}) conditional(s32[]{:T(128)} %convert_element_type.42, (s32[]{:T(128)}, pred[16,14,192]{2,1,0:T(8,128)(4,1)S(1)}, s32[192]{0:T(256)S(1)}, s32[12]{0:T(128)S(1)}, s32[12]{0:T(128)S(1)}, /*index=5*/s32[192]{0:T(256)S(1)}, s32[12]{0:T(128)S(1)}, s32[24]{0:T(128)S(1)}, s32[24]{0:T(128)S(1)}, ...), branch_computations={%region_6.12_spmd, %region_12.26_spmd} | conditional | flops 520247 | bytes 2463457 | solution.py:331
  65.6 0.1 select_reduce_fusion.3
  65.7 0.1 pad_add_fusion.1
  65.8 0.1 broadcast_compare_fusion.3
  65.9 0.1 compare_and_fusion
  65.9 0.1 add_multiply_fusion
  66.0 0.1 broadcast_compare_fusion
  66.1 0.1 broadcast_compare_fusion.2
  66.2 0.1 select_reduce_fusion
  66.3 0.1 convert_reduce_fusion
  66.4 0.1 fusion.1
  66.6 0.3 select_reduce_fusion.1.listed
  66.8 3.0 %multiply.6 = f32[12,128,128]{2,1,0:T(8,128)} custom-call(s32[12]{0:T(128)S(1)} %get-tuple-element.363.counts, s32[12,16]{1,0:T(8,128)S(1)} %select_reduce_fusion.1.listed, f32[14,128,128]{2,1,0:T(8,128)S(1)} %get-tuple-element.277.arrived, f32[24,128,128]{2,1,0:T(8,128)S(1)} %get-tuple-element.278.panel), custom_call_target="tpu_custom_call" | custom-call | tf_op jit(solution)/shard_map/cond/branch_0_fun/multiply/pallas_call | solution.py:307
  (13 shorter events, 0.1 us)

commit v3 on v2

--- a/solution.py
+++ b/solution.py
@@ -2,6 +2,7 @@
 
 import jax
 import jax.numpy as jnp
+import numpy as np
 from jax import lax
 from jax.experimental import pallas as pl
 from jax.experimental.pallas import tpu as pltpu
@@ -47,8 +48,10 @@
     lists, slots = rows.shape
     layers, kept = goal_rows.shape
     meta[...] = jnp.zeros_like(meta)
-    live = lax.broadcasted_iota(jnp.int32, (lists, slots), 1) < counts[...]
-    meta[0:lists, 0:slots] = jnp.where(live, rows[...], -1)
+    slot = lax.broadcasted_iota(jnp.int32, (1, slots), 1)
+    for h in range(lists):
+        live = slot < counts[0:1, h : h + 1]
+        meta[h : h + 1, 0:slots] = jnp.where(live, rows[h : h + 1, :], -1)
     meta[lists : 2 * lists, 0:slots] = cols[...]
     meta[2 * lists : 2 * lists + layers, 0:kept] = goal_rows[...]
     meta[2 * lists + layers : 2 * lists + 2 * layers, 0:kept] = goal_cols[...]
@@ -83,8 +86,8 @@
     own_meta = pltpu.make_async_copy(meta, meta_all.at[flat], local_sem.at[0])
     own_slice = pltpu.make_async_copy(tiles.at[:, sub], landed.at[sub], local_sem.at[1])
     own_panel = pltpu.make_async_copy(tiles, panel.at[row], local_sem.at[2])
-    each(n_sub - 1, lambda k: slice_copy(far_first(k - 1, n_sub)).start())
     each(total - 1, lambda k: meta_copy(k).start())
+    each(n_sub - 1, lambda k: slice_copy(k).start())
     each(n_row - 1, lambda k: panel_copy(k).start())
     own_meta.start()
     own_slice.start()
@@ -170,7 +173,7 @@
 
 def running_count(flags):
     size = flags.shape[-1]
-    upper = (jnp.arange(size)[:, None] <= jnp.arange(size)[None, :]).astype(jnp.bfloat16)
+    upper = jnp.asarray(np.triu(np.ones((size, size), np.float32)), jnp.bfloat16)
     return jnp.dot(flags.astype(jnp.bfloat16), upper,
                    preferred_element_type=jnp.float32).astype(jnp.int32)
 
@@ -187,7 +190,6 @@
     sub = lax.axis_index("col") * n_layer + layer
 
     tiles = tile_values.reshape(slots, n_sub, part, order)
-    own_cols = tile_cols.reshape(-1)
     lists = tile_rows.shape[2]
 
     anywhere = pl.BlockSpec(memory_space=pl.ANY)
@@ -212,7 +214,7 @@
         ],
         compiler_params=pltpu.CompilerParams(collective_id=1, has_side_effects=True),
         name="spread",
-    )(tiles, tile_rows[0, 0], tile_cols[0, 0], tile_counts.reshape(lists, 1),
+    )(tiles, tile_rows[0, 0], tile_cols[0, 0], tile_counts[0],
       out_rows[0, 0], out_cols[0, 0])
     landed = landed.reshape(n_sub * slots, part, order)
     panel = panel.reshape(n_row * slots, order, order)
@@ -224,10 +226,10 @@
     goals = lines[:, :, 0, 2 * lists : 2 * lists + 2 * n_layer, :kept]
     goal_rows = goals[:, :, :n_layer].reshape(n_row, n_sub, kept)
     goal_cols = goals[:, :, n_layer:].reshape(n_row, n_sub, kept)
-    live = jnp.arange(per_list) < tile_counts[0, 0][:, None]
-    own_rows = jnp.where(live, tile_rows[0, 0], -1).reshape(-1)
-    target_rows = lax.dynamic_index_in_dim(out_rows[0, 0], layer, 0, keepdims=False)
-    target_cols = lax.dynamic_index_in_dim(out_cols[0, 0], layer, 0, keepdims=False)
+    own_rows = list_rows[row, sub]
+    own_cols = list_cols[row, sub]
+    target_rows = goal_rows[row, sub]
+    target_cols = goal_cols[row, sub]
     bits = jnp.left_shift(1, jnp.arange(kept, dtype=jnp.int32))
     left_rows = list_rows.reshape(n_row, n_sub * slots)
     left_cols = list_cols.reshape(n_row, n_sub * slots)
@@ -276,7 +278,7 @@
             ],
             compiler_params=pltpu.CompilerParams(
                 collective_id=collective_id, has_side_effects=True,
-                vmem_limit_bytes=16 * 1024 * 1024),
+                vmem_limit_bytes=32 * 1024 * 1024),
             name="deliver",
         )(wanted, landed)
         return arrived.reshape(ROUND, order, order), chosen
@@ -314,21 +316,18 @@
                 pl.BlockSpec(memory_space=pltpu.VMEM),
             ],
             out_specs=pl.BlockSpec(memory_space=pltpu.VMEM),
-            compiler_params=pltpu.CompilerParams(vmem_limit_bytes=16 * 1024 * 1024),
+            compiler_params=pltpu.CompilerParams(vmem_limit_bytes=32 * 1024 * 1024),
             name="multiply",
         )(counts, listed, arrived, panel)
 
     arrived, chosen = deliver(0, 2)
 
-    def more_rounds():
-        def again(state):
-            turn, so_far = state
-            return turn + 1, so_far + products(turn, *deliver(turn, 3))
-
-        start = (jnp.int32(1), products(0, arrived, chosen))
-        return lax.while_loop(lambda state: state[0] < rounds, again, start)[1]
-
-    summed = lax.cond(rounds > 1, more_rounds, lambda: products(0, arrived, chosen))
+    def again(state):
+        turn, so_far = state
+        return turn + 1, so_far + products(turn, *deliver(turn, 3))
+
+    start = (jnp.int32(1), products(0, arrived, chosen))
+    summed = lax.while_loop(lambda state: state[0] < rounds, again, start)[1]
     return summed.reshape(1, 1, kept, order, order)
 
 

time: 70.3 us -> 66.2 us (0.942)
  local copies, waits for them, and re-layouts: 6.25 us -> 3.56 us
  other arithmetic: 3.65 us -> 2.91 us
    pallas_call x1, Pallas kernels: 29.9 us -> 24.1 us  [local(): pl.pallas_call(functools.partial(spread_kernel, n_row, n_sub, n_layer), o...]
    pallas_call x1, Pallas kernels: 25.9 us -> 31.1 us  [deliver(): pl.pallas_call(functools.partial(deliver_kernel, n_sub, n_layer), out_sha...]
    reshape x2 -> x0, local copies, waits for them, and re-layouts: 2.05 us -> none  [the longest x1 1.3 us: local(): tile_counts.reshape(lists, 1)]
    squeeze x3 -> x2, local copies, waits for them, and re-layouts: 1.47 us -> 0.01 us  [the longest x1 0.01 us: local(): own_rows = list_rows[row, sub]]
    unnamed x0 -> x6, local copies, waits for them, and re-layouts: none -> 0.88 us
    lt x1 -> x0, other arithmetic: 0.73 us -> none  [local(): live = jnp.arange(per_list) < tile_counts[0, 0][:, None]]
where the time goes in v3:
time: 66.2 us; the launch traced here: 65.9 us
  Pallas kernels  58.3 us (88%)
  local copies, waits for them, and re-layouts  3.56 us (5%)
  other arithmetic  2.91 us (4%)
  between operations  0.89 us (1%)
    pallas_call x1, Pallas kernels, deliver(): pl.pallas_call(functools.partial(deliver_kernel, n_sub, n_layer), out_sha...  31.1 us
    pallas_call x1, Pallas kernels, local(): pl.pallas_call(functools.partial(spread_kernel, n_row, n_sub, n_layer), o...  24.1 us
    pallas_call x1, Pallas kernels, products(): pl.pallas_call(functools.partial(multiply_kernel, base), out_shape=jax.Sh...  3.07 us

profile of v3, /device:TPU:0, one launch (start us, length us, event | category | flops | bytes accessed | tf_op | source)
XLA Modules:
  0.0 65.9 jit_solution(5691098263690161336)
XLA Ops:
  0.0 0.0 copy-start.2
  0.0 0.0 copy-start.1
  0.1 24.1 %spread.1 = (f32[16,12,8,128]{3,2,1,0:T(8,128)S(1)}, f32[2,12,16,8,128]{4,3,2,1,0:T(8,128)S(1)}, s32[32,8,128]{2,1,0:T(8,128)}) custom-call(f32[12,16,8,128]{3,2,1,0:T(8,128)} %bitcast.64, s32[2,6]{1,0:T(2,128)} %bitcast.81, s32[2,6]{1,0:T(2,128)} %bitcast.82, s32[1,2]{1,0:T(1,128)} %bitcast.85, s32[2,12]{1,0:T(2,128)} %bitcast.83, s32[2,12]{1,0:T(2,128)} %bitcast.84), custom_call_target="tpu_custom_call" | custom-call | tf_op jit(solution)/shard_map/spread/pallas_call | solution.py:196
  24.2 0.8 %slice_bitcast_fusion = s32[2,8,4,12]{3,2,1,0:T(4,128)S(1)} fusion(s32[2,8,2,8,128]{4,3,2,1,0:T(8,128)} %bitcast.65), kind=kLoop, calls=%fused_computation.41 | loop fusion | bytes 6144 | tf_op jit(solution)/shard_map/squeeze | solution.py:226
  25.0 1.0 %fusion.18 = (s32[2,8,2,2,6]{4,3,2,1,0:T(2,128)S(1)}, s32[2,8,2,2,6]{4,3,2,1,0:T(2,128)S(1)}) fusion(s32[2,8,2,8,128]{4,3,2,1,0:T(8,128)} %bitcast.66), kind=kLoop, calls=%fused_computation.78 | loop fusion | bytes 6144 | tf_op jit(solution)/shard_map/slice | solution.py:224
  26.1 0.1 copy.23
  26.2 0.1 copy.25
  26.2 0.1 eq.257
  26.4 0.1 reshape.412
  26.5 0.1 eq.254
  26.6 0.1 reshape.413
  26.7 0.1 select_reduce_fusion.4
  26.8 0.1 eq.262
  26.9 0.1 select_reduce_fusion.6
  27.1 0.1 eq.252
  27.2 0.4 fusion.10
  27.5 0.1 convert_reduce_fusion.1
  27.7 0.7 %reduce_max.75 = s32[]{:T(128)} reduce(s32[2,16]{1,0:T(2,128)S(1)} %get-tuple-element.371, s32[]{:T(128)} %constant.123.clone.1), dimensions={0,1}, to_apply=%region_10.11 | reduce | flops 31 | bytes 136 | tf_op jit(solution)/shard_map/reduce_max | solution.py:248
  29.1 0.1 broadcast_compare_fusion.7
  29.2 0.0 copy-done.2
  29.2 0.1 fusion.6
  29.3 0.4 select_reduce_fusion.5.wanted
  29.7 0.1 select_reduce_fusion.10
  29.9 0.1 pad_add_fusion.3
  29.9 0.1 broadcast_compare_fusion.8
  30.0 0.1 compare_and_fusion.1
  30.1 0.1 broadcast_compare_fusion.5
  30.2 0.1 select_reduce_fusion.7
  30.3 0.1 convert_reduce_fusion.2
  30.4 0.0 copy-done.1
  30.4 0.1 fusion.8
  30.5 0.3 select_reduce_fusion.8.listed
  30.8 31.1 %deliver.5 = f32[14,16,8,128]{3,2,1,0:T(8,128)S(1)} custom-call(s32[16,14]{1,0:T(8,128)S(1)} %select_reduce_fusion.5.wanted, f32[192,8,128]{2,1,0:T(8,128)S(1)} %bitcast.62), custom_call_target="tpu_custom_call" | custom-call | tf_op jit(solution)/shard_map/deliver/pallas_call | solution.py:265
  61.9 3.1 %multiply.5 = f32[12,128,128]{2,1,0:T(8,128)S(1)} custom-call(s32[12]{0:T(128)S(1)} %get-tuple-element.373.counts, s32[12,16]{1,0:T(8,128)S(1)} %select_reduce_fusion.8.listed, f32[14,128,128]{2,1,0:T(8,128)S(1)} %bitcast.59, f32[24,128,128]{2,1,0:T(8,128)S(1)} %bitcast.60), custom_call_target="tpu_custom_call" | custom-call | tf_op jit(solution)/shard_map/multiply/pallas_call | solution.py:309
  65.0 0.0 copy-start
  65.1 0.9 %copy-done = f32[12,128,128]{2,1,0:T(8,128)} copy-done((f32[12,128,128]{2,1,0:T(8,128)}, f32[12,128,128]{2,1,0:T(8,128)S(1)}, u32[]{:S(2)}) %copy-start) | copy-done | bytes 786456
  (16 shorter events, 0.2 us)
Async XLA Ops:
  0.0 29.2 %copy-start.2 = (bf16[192,192]{1,0:T(8,128)(2,1)S(1)}, bf16[192,192]{1,0:T(8,128)(2,1)}, u32[]{:S(2)}) copy-start(bf16[192,192]{1,0:T(8,128)(2,1)} %constant.127.clone) | copy-start | bytes 221188
  0.0 30.4 %copy-start.1 = (bf16[26,26]{1,0:T(8,128)(2,1)S(1)}, bf16[26,26]{1,0:T(8,128)(2,1)}, u32[]{:S(2)}) copy-start(bf16[26,26]{1,0:T(8,128)(2,1)} %constant.128.clone) | copy-start | bytes 4060
  65.0 0.9 %copy-start = (f32[12,128,128]{2,1,0:T(8,128)}, f32[12,128,128]{2,1,0:T(8,128)S(1)}, u32[]{:S(2)}) copy-start(f32[12,128,128]{2,1,0:T(8,128)S(1)} %get-tuple-element.240) | copy-start | bytes 2359300

commit v4 on v3

--- a/solution.py
+++ b/solution.py
@@ -21,10 +21,6 @@
 
     lax.fori_loop(0, count, step, 0)
     pl.semaphore_wait(barrier, count)
-
-
-def far_first(k, n_sub):
-    return n_sub // 2 + (1 - 2 * ((k + 1) % 2)) * ((k + 1) // 2)
 
 
 def spread_kernel(
@@ -51,10 +47,14 @@
     slot = lax.broadcasted_iota(jnp.int32, (1, slots), 1)
     for h in range(lists):
         live = slot < counts[0:1, h : h + 1]
-        meta[h : h + 1, 0:slots] = jnp.where(live, rows[h : h + 1, :], -1)
-    meta[lists : 2 * lists, 0:slots] = cols[...]
-    meta[2 * lists : 2 * lists + layers, 0:kept] = goal_rows[...]
-    meta[2 * lists + layers : 2 * lists + 2 * layers, 0:kept] = goal_cols[...]
+        meta[:, h * slots : (h + 1) * slots] = jnp.where(live, rows[h : h + 1, :], -1)
+        start = (lists + h) * slots
+        meta[:, start : start + slots] = cols[h : h + 1, :]
+    for at in range(layers):
+        start = 2 * lists * slots + at * kept
+        meta[:, start : start + kept] = goal_rows[at : at + 1, :]
+        start += layers * kept
+        meta[:, start : start + kept] = goal_cols[at : at + 1, :]
 
     def meta_copy(k):
         return pltpu.make_async_remote_copy(
@@ -120,7 +120,7 @@
             recv_sem=recv_sem.at[k], device_id=device_of(place), device_id_type=MESH)
 
     def out_step(k, unused):
-        shift = far_first(k, n_sub)
+        shift = k + 1
         pack(lax.rem(sub + shift, n_sub))
         send(shift).start()
         return unused
@@ -198,12 +198,12 @@
         out_shape=(
             jax.ShapeDtypeStruct((n_sub, slots, part, order), jnp.float32),
             jax.ShapeDtypeStruct((n_row, slots, n_sub, part, order), jnp.float32),
-            jax.ShapeDtypeStruct((total, 8, 128), jnp.int32),
+            jax.ShapeDtypeStruct((total, 1, 128), jnp.int32),
         ),
         in_specs=[anywhere] + [pl.BlockSpec(memory_space=pltpu.VMEM)] * 5,
         out_specs=(anywhere, anywhere, anywhere),
         scratch_shapes=[
-            pltpu.VMEM((8, 128), jnp.int32),
+            pltpu.VMEM((1, 128), jnp.int32),
             pltpu.SemaphoreType.DMA((n_sub,)),
             pltpu.SemaphoreType.DMA((n_sub,)),
             pltpu.SemaphoreType.DMA((n_row,)),
@@ -219,13 +219,16 @@
     landed = landed.reshape(n_sub * slots, part, order)
     panel = panel.reshape(n_row * slots, order, order)
 
-    lines = meta_all.reshape(n_row, n_col, n_layer, 8, 128)
-    per_list = slots // lists
-    list_rows = lines[..., 0:lists, :per_list].reshape(n_row, n_sub, slots)
-    list_cols = lines[..., lists : 2 * lists, :per_list].reshape(n_row, n_sub, slots)
-    goals = lines[:, :, 0, 2 * lists : 2 * lists + 2 * n_layer, :kept]
-    goal_rows = goals[:, :, :n_layer].reshape(n_row, n_sub, kept)
-    goal_cols = goals[:, :, n_layer:].reshape(n_row, n_sub, kept)
+    lines = meta_all.reshape(n_row, n_sub, 128)
+    list_rows = lines[:, :, :slots]
+    list_cols = lines[:, :, slots : 2 * slots]
+    odd = jnp.arange(n_sub)[:, None] % n_layer
+    goal_rows, goal_cols = 0, 0
+    for at in range(n_layer):
+        start = 2 * slots + at * kept
+        goal_rows = jnp.where(odd == at, lines[:, :, start : start + kept], goal_rows)
+        start += n_layer * kept
+        goal_cols = jnp.where(odd == at, lines[:, :, start : start + kept], goal_cols)
     own_rows = list_rows[row, sub]
     own_cols = list_cols[row, sub]
     target_rows = goal_rows[row, sub]

time: 66.2 us -> 62 us (0.937)
  the two profiles are of different devices: /device:TPU:0 before, /device:TPU:10 now
where the time goes in v4:
time: 62 us; the launch traced here: 61.9 us
  Pallas kernels  54.4 us (88%)
  other arithmetic  3.96 us (6%)
  local copies, waits for them, and re-layouts  1.48 us (2%)
  matrix products  1.15 us (2%)
  between operations  0.91 us (1%)
    pallas_call x1, Pallas kernels, deliver(): pl.pallas_call(functools.partial(deliver_kernel, n_sub, n_layer), out_sha...  26.4 us
    pallas_call x1, Pallas kernels, local(): pl.pallas_call(functools.partial(spread_kernel, n_row, n_sub, n_layer), o...  24.9 us
    pallas_call x1, Pallas kernels, products(): pl.pallas_call(functools.partial(multiply_kernel, base), out_shape=jax.Sh...  3.07 us

profile of v4, /device:TPU:10, one launch (start us, length us, event | category | flops | bytes accessed | tf_op | source)
XLA Modules:
  0.0 61.9 jit_solution(10562044679745755982)
XLA Ops:
  0.0 0.0 copy-start.1
  0.1 24.9 %spread.1 = (f32[16,12,8,128]{3,2,1,0:T(8,128)S(1)}, f32[2,12,16,8,128]{4,3,2,1,0:T(8,128)S(1)}, s32[32,1,128]{2,1,0:T(1,128)}) custom-call(f32[12,16,8,128]{3,2,1,0:T(8,128)} %bitcast.62, s32[2,6]{1,0:T(2,128)} %bitcast.72, s32[2,6]{1,0:T(2,128)} %bitcast.73, s32[1,2]{1,0:T(1,128)} %bitcast.76, s32[2,12]{1,0:T(2,128)} %bitcast.74, s32[2,12]{1,0:T(2,128)} %bitcast.75), custom_call_target="tpu_custom_call" | custom-call | tf_op jit(solution)/shard_map/spread/pallas_call | solution.py:196
  25.0 1.0 %slice_bitcast_fusion.1 = (s32[16,2,12]{2,0,1:T(8,128)S(1)}, s32[16,2,12]{2,0,1:T(8,128)S(1)}, s32[2,16,12]{2,1,0:T(8,128)S(1)}, s32[2,16,12]{2,1,0:T(8,128)S(1)...) fusion(s32[2,16,128]{2,1,0:T(8,128)} %bitcast.63, pred[16]{0:T(512)(128)(4,1)S(1)} %broadcast_compare_fusion.9, ...), kind=kLoop, calls=%fused_computation.85 | loop fusion | flops 1536 | bytes 18464 | tf_op jit(solution)/shard_map/transpose | solution.py:239
  26.1 0.1 eq.268
  26.1 0.1 eq.270
  26.3 0.1 eq.273
  26.4 0.1 copy.21
  26.5 0.1 copy.23
  26.6 0.1 select_reduce_fusion.4
  26.7 0.1 eq.279
  26.8 0.1 select_reduce_fusion.6
  26.9 0.4 fusion.10
  27.3 0.1 convert_reduce_fusion.1
  27.4 0.7 %reduce_max.75 = s32[]{:T(128)} reduce(s32[2,16]{1,0:T(2,128)S(1)} %get-tuple-element.371, s32[]{:T(128)} %constant.137.clone.1), dimensions={0,1}, to_apply=%region_10.11 | reduce | flops 31 | bytes 136 | tf_op jit(solution)/shard_map/reduce_max | solution.py:251
  28.9 0.1 broadcast_compare_fusion.7
  29.0 1.0 %fusion.6 = s32[16,192]{1,0:T(8,128)S(1)} fusion(bf16[192,192]{1,0:T(8,128)(2,1)} %constant.141.clone, pred[2,16,192]{2,1,0:T(8,128)(4,1)S(1)} %get-tuple-element.372, s32[]{:T(128)S(6)} %select_n.177), kind=kOutput, calls=%fused_computation.27 | convolution fusion | flops 1188864 | bytes 93184 | tf_op jit(solution)/shard_map/dot_general | solution.py:177
  30.0 0.4 select_reduce_fusion.5.wanted
  30.4 0.1 select_reduce_fusion.10
  30.5 0.1 pad_add_fusion.3
  30.6 0.1 broadcast_compare_fusion.8
  30.7 0.1 compare_and_fusion.1
  30.8 0.1 broadcast_compare_fusion.5
  30.8 0.1 select_reduce_fusion.7
  31.0 0.1 convert_reduce_fusion.2
  31.1 0.0 copy-done.1
  31.1 0.1 fusion.8
  31.2 0.3 select_reduce_fusion.8.listed
  31.5 26.4 %deliver.5 = f32[14,16,8,128]{3,2,1,0:T(8,128)S(1)} custom-call(s32[16,14]{1,0:T(8,128)S(1)} %select_reduce_fusion.5.wanted, f32[192,8,128]{2,1,0:T(8,128)S(1)} %bitcast.60), custom_call_target="tpu_custom_call" | custom-call | tf_op jit(solution)/shard_map/deliver/pallas_call | solution.py:268
  57.9 3.1 %multiply.5 = f32[12,128,128]{2,1,0:T(8,128)S(1)} custom-call(s32[12]{0:T(128)S(1)} %get-tuple-element.373.counts, s32[12,16]{1,0:T(8,128)S(1)} %select_reduce_fusion.8.listed, f32[14,128,128]{2,1,0:T(8,128)S(1)} %bitcast.57, f32[24,128,128]{2,1,0:T(8,128)S(1)} %bitcast.58), custom_call_target="tpu_custom_call" | custom-call | tf_op jit(solution)/shard_map/multiply/pallas_call | solution.py:312
  61.0 0.0 copy-start
  61.0 0.9 %copy-done = f32[12,128,128]{2,1,0:T(8,128)} copy-done((f32[12,128,128]{2,1,0:T(8,128)}, f32[12,128,128]{2,1,0:T(8,128)S(1)}, u32[]{:S(2)}) %copy-start) | copy-done | bytes 786456
  (17 shorter events, 0.2 us)
Async XLA Ops:
  0.0 31.1 %copy-start.1 = (bf16[26,26]{1,0:T(8,128)(2,1)S(1)}, bf16[26,26]{1,0:T(8,128)(2,1)}, u32[]{:S(2)}) copy-start(bf16[26,26]{1,0:T(8,128)(2,1)} %constant.142.clone) | copy-start | bytes 4060
  61.0 0.9 %copy-start = (f32[12,128,128]{2,1,0:T(8,128)}, f32[12,128,128]{2,1,0:T(8,128)S(1)}, u32[]{:S(2)}) copy-start(f32[12,128,128]{2,1,0:T(8,128)S(1)} %get-tuple-element.240) | copy-start | bytes 2359300

commit v5 on v4

--- a/solution.py
+++ b/solution.py
@@ -21,6 +21,10 @@
 
     lax.fori_loop(0, count, step, 0)
     pl.semaphore_wait(barrier, count)
+
+
+def both_ways(k, n_sub):
+    return (1 - k % 2) * (1 + k // 2) + (k % 2) * (n_sub - (k + 1) // 2)
 
 
 def spread_kernel(
@@ -87,7 +91,7 @@
     own_slice = pltpu.make_async_copy(tiles.at[:, sub], landed.at[sub], local_sem.at[1])
     own_panel = pltpu.make_async_copy(tiles, panel.at[row], local_sem.at[2])
     each(total - 1, lambda k: meta_copy(k).start())
-    each(n_sub - 1, lambda k: slice_copy(k).start())
+    each(n_sub - 1, lambda k: slice_copy(both_ways(k - 1, n_sub)).start())
     each(n_row - 1, lambda k: panel_copy(k).start())
     own_meta.start()
     own_slice.start()
@@ -120,7 +124,7 @@
             recv_sem=recv_sem.at[k], device_id=device_of(place), device_id_type=MESH)
 
     def out_step(k, unused):
-        shift = k + 1
+        shift = both_ways(k, n_sub)
         pack(lax.rem(sub + shift, n_sub))
         send(shift).start()
         return unused

time: 62 us -> 63.6 us (1.026)
  the two profiles are of different devices: /device:TPU:10 before, /device:TPU:0 now
where the time goes in v5:
time: 63.6 us; the launch traced here: 63.2 us
  Pallas kernels  55.7 us (88%)
  other arithmetic  3.96 us (6%)
  local copies, waits for them, and re-layouts  1.48 us (2%)
  matrix products  1.15 us (2%)
  between operations  0.9 us (1%)
    pallas_call x1, Pallas kernels, local(): pl.pallas_call(functools.partial(spread_kernel, n_row, n_sub, n_layer), o...  28.4 us
    pallas_call x1, Pallas kernels, deliver(): pl.pallas_call(functools.partial(deliver_kernel, n_sub, n_layer), out_sha...  24.5 us
    pallas_call x1, Pallas kernels, products(): pl.pallas_call(functools.partial(multiply_kernel, base), out_shape=jax.Sh...  2.88 us

profile of v5, /device:TPU:0, one launch (start us, length us, event | category | flops | bytes accessed | tf_op | source)
XLA Modules:
  0.0 63.2 jit_solution(3064264345312642193)
XLA Ops:
  0.0 0.0 copy-start.1
  0.1 28.4 %spread.1 = (f32[16,12,8,128]{3,2,1,0:T(8,128)S(1)}, f32[2,12,16,8,128]{4,3,2,1,0:T(8,128)S(1)}, s32[32,1,128]{2,1,0:T(1,128)}) custom-call(f32[12,16,8,128]{3,2,1,0:T(8,128)} %bitcast.62, s32[2,6]{1,0:T(2,128)} %bitcast.72, s32[2,6]{1,0:T(2,128)} %bitcast.73, s32[1,2]{1,0:T(1,128)} %bitcast.76, s32[2,12]{1,0:T(2,128)} %bitcast.74, s32[2,12]{1,0:T(2,128)} %bitcast.75), custom_call_target="tpu_custom_call" | custom-call | tf_op jit(solution)/shard_map/spread/pallas_call | solution.py:200
  28.4 1.0 %slice_bitcast_fusion.1 = (s32[16,2,12]{2,0,1:T(8,128)S(1)}, s32[16,2,12]{2,0,1:T(8,128)S(1)}, s32[2,16,12]{2,1,0:T(8,128)S(1)}, s32[2,16,12]{2,1,0:T(8,128)S(1)...) fusion(s32[2,16,128]{2,1,0:T(8,128)} %bitcast.63, pred[16]{0:T(512)(128)(4,1)S(1)} %broadcast_compare_fusion.9, ...), kind=kLoop, calls=%fused_computation.85 | loop fusion | flops 1536 | bytes 18464 | tf_op jit(solution)/shard_map/transpose | solution.py:243
  29.5 0.1 eq.268
  29.6 0.1 eq.270
  29.7 0.1 eq.273
  29.8 0.1 copy.21
  29.9 0.1 copy.23
  30.0 0.1 select_reduce_fusion.4
  30.2 0.1 eq.279
  30.3 0.1 select_reduce_fusion.6
  30.4 0.4 fusion.10
  30.8 0.1 convert_reduce_fusion.1
  30.9 0.7 %reduce_max.75 = s32[]{:T(128)} reduce(s32[2,16]{1,0:T(2,128)S(1)} %get-tuple-element.371, s32[]{:T(128)} %constant.137.clone.1), dimensions={0,1}, to_apply=%region_10.11 | reduce | flops 31 | bytes 136 | tf_op jit(solution)/shard_map/reduce_max | solution.py:255
  32.3 0.1 broadcast_compare_fusion.7
  32.4 1.0 %fusion.6 = s32[16,192]{1,0:T(8,128)S(1)} fusion(bf16[192,192]{1,0:T(8,128)(2,1)} %constant.141.clone, pred[2,16,192]{2,1,0:T(8,128)(4,1)S(1)} %get-tuple-element.372, s32[]{:T(128)S(6)} %select_n.177), kind=kOutput, calls=%fused_computation.27 | convolution fusion | flops 1188864 | bytes 93184 | tf_op jit(solution)/shard_map/dot_general | solution.py:181
  33.4 0.4 select_reduce_fusion.5.wanted
  33.9 0.1 select_reduce_fusion.10
  34.0 0.1 pad_add_fusion.3
  34.1 0.1 broadcast_compare_fusion.8
  34.1 0.1 compare_and_fusion.1
  34.2 0.1 broadcast_compare_fusion.5
  34.3 0.1 select_reduce_fusion.7
  34.4 0.1 convert_reduce_fusion.2
  34.5 0.0 copy-done.1
  34.5 0.1 fusion.8
  34.7 0.3 select_reduce_fusion.8.listed
  35.0 24.5 %deliver.5 = f32[14,16,8,128]{3,2,1,0:T(8,128)S(1)} custom-call(s32[16,14]{1,0:T(8,128)S(1)} %select_reduce_fusion.5.wanted, f32[192,8,128]{2,1,0:T(8,128)S(1)} %bitcast.60), custom_call_target="tpu_custom_call" | custom-call | tf_op jit(solution)/shard_map/deliver/pallas_call | solution.py:272
  59.4 2.9 %multiply.5 = f32[12,128,128]{2,1,0:T(8,128)S(1)} custom-call(s32[12]{0:T(128)S(1)} %get-tuple-element.373.counts, s32[12,16]{1,0:T(8,128)S(1)} %select_reduce_fusion.8.listed, f32[14,128,128]{2,1,0:T(8,128)S(1)} %bitcast.57, f32[24,128,128]{2,1,0:T(8,128)S(1)} %bitcast.58), custom_call_target="tpu_custom_call" | custom-call | tf_op jit(solution)/shard_map/multiply/pallas_call | solution.py:316
  62.3 0.0 copy-start
  62.4 0.9 %copy-done = f32[12,128,128]{2,1,0:T(8,128)} copy-done((f32[12,128,128]{2,1,0:T(8,128)}, f32[12,128,128]{2,1,0:T(8,128)S(1)}, u32[]{:S(2)}) %copy-start) | copy-done | bytes 786456
  (17 shorter events, 0.2 us)
Async XLA Ops:
  0.0 34.5 %copy-start.1 = (bf16[26,26]{1,0:T(8,128)(2,1)S(1)}, bf16[26,26]{1,0:T(8,128)(2,1)}, u32[]{:S(2)}) copy-start(bf16[26,26]{1,0:T(8,128)(2,1)} %constant.142.clone) | copy-start | bytes 4060
  62.3 0.9 %copy-start = (f32[12,128,128]{2,1,0:T(8,128)}, f32[12,128,128]{2,1,0:T(8,128)S(1)}, u32[]{:S(2)}) copy-start(f32[12,128,128]{2,1,0:T(8,128)S(1)} %get-tuple-element.240) | copy-start | bytes 2359300
